TPU v7x, 32 devices: a whole 2x2x4 slice. The times are simulated.
32 devices in a mesh: line: 4 (over z), bus: 4 (over y, core), tm: 2 (over x).
Axes of the slice: x: 2, y: 2, z: 4, core: 2. Of those that a mesh axis runs over, the one named last changes fastest.
Arguments:
- ptdf_matrix: float32 [15360, 12288], P('line', 'bus'), may hold values from -0.0546875 to 0.0546875
- bus_load: float32 [12288, 256], P('bus', 'tm'), may hold values from 0 to 1
- unit_bus: int32 [4096], P(('line', 'bus')), may hold values from 0 to 12287, as said below
- unit_type: int32 [4096], P(('line', 'bus')), may hold values from 0 to 3
- unit_limit: int32 [4096], P(('line', 'bus')), may hold values from 50 to 499
- unit_cost: float32 [4096], P(('line', 'bus')), may hold values from 0.1 to 1
- line_rating: int32 [15360], P('line'), may hold values from 20 to 299
Outputs:
- generation: float32 [4096, 256], P(('line', 'bus'), 'tm')
- line_dual: float32 [15360, 256], P('line', 'tm')
Inputs may be any that keep to these rules, and one draw needn't show every extreme that they name: `unit_bus`: let G be the number of devices of line and bus together, U = 4096 / G and S = 12288 / G. Unit u lies in group q = u // U; it sits at a bus of the S consecutive buses that begin at (q mod the size of bus) * 12288 / (size of bus) + (q // size of bus) * S.
All inputs are finite; a program needn't handle non-finite values.
Results may differ from a plain program's by a relative error of at most 0.0003.
Values sent between devices are 32-bit elements; how exact they have to be, the bound alone decides.
A program may use at most 192 MiB of HBM per device.

v0:
```python
import functools

import jax
import jax.numpy as jnp
from jax import lax
from jax.experimental import pallas as pl
from jax.experimental.pallas import tpu as pltpu
from jax.sharding import PartitionSpec as P

UNITS = 4096
ITERS = 4
MESH = pl.DeviceIdType.MESH


RAMP_RATES = (0.1, 0.2, 0.4, 0.5)
COST_FACTORS = (1.0, 1.5, 3.0, 0.05)
PRIMAL_STEP = 0.5
DUAL_STEP = 0.5


def unit_tables(unit_type, unit_limit, unit_cost):
    capacity = unit_limit.astype(jnp.float32) / 100.0
    kinds = (unit_type[:, None] == jnp.arange(4, dtype=jnp.int32)[None, :]).astype(jnp.float32)
    rates = jnp.sum(kinds * jnp.array(RAMP_RATES, jnp.float32)[None, :], axis=1)
    factors = jnp.sum(kinds * jnp.array(COST_FACTORS, jnp.float32)[None, :], axis=1)
    storage = kinds[:, 3]
    return (
        unit_cost * factors,
        -capacity * storage,
        capacity,
        rates * capacity,
        storage,
        2.0 * capacity,
    )


def parts(value):
    high = lax.reduce_precision(value, 8, 7)
    return high.astype(jnp.bfloat16), (value - high).astype(jnp.bfloat16)


def exact(left, right):
    return jnp.dot(left, right, precision=lax.Precision.HIGHEST, preferred_element_type=jnp.float32)


def shifted(value, axis, by):
    length = lax.axis_size(axis)
    pairs = [(i, i + by) for i in range(length) if 0 <= i + by < length]
    return lax.ppermute(value, axis, pairs)


def gathered(edge, total, axis, sign):
    edge_there, total_there = jnp.zeros_like(edge), jnp.zeros_like(total)
    for k in range(1, lax.axis_size(axis)):
        if k == 1:
            both = shifted(jnp.stack([edge, total]), axis, sign)
            edge_there, total_there = both[0], both[1]
        else:
            total_there = total_there + shifted(total, axis, sign * k)
    return edge_there, total_there


def stages(steps, tile, part, there, chips, done, sems):
    a_send, a_recv, b_send, b_recv, c_send, c_recv = sems
    bus = lax.axis_index("bus")
    chip_count = chips.shape[0]
    core, chip = lax.rem(bus, 2), lax.div(bus, 2)
    sibling = bus + 1 - 2 * core
    pairs = steps // 2
    half = pairs * tile
    mine, other = core * half, (1 - core) * half
    partners = [lax.rem(chip + j, chip_count) * 2 + core for j in range(1, chip_count)]

    def rows(begin, size):
        return pl.ds(pl.multiple_of(begin, 8), size)

    def copy(source, target, send_sem, recv_sem, peer):
        return pltpu.make_async_remote_copy(
            src_ref=source,
            dst_ref=target,
            send_sem=send_sem,
            recv_sem=recv_sem,
            device_id={"bus": peer},
            device_id_type=MESH,
        )

    def size_of(k):
        return 8 if isinstance(k, int) and k == pairs else tile

    def first(k):
        begin = 2 * half if isinstance(k, int) and k == pairs else other + k * tile
        return copy(
            part.at[rows(begin, size_of(k))],
            there.at[rows(k * tile, size_of(k))],
            a_send.at[k], a_recv.at[k], sibling,
        )

    def cross(k):
        place = chips.at[chip, rows(k * tile, size_of(k))]
        return [
            copy(place, place, b_send.at[j, k], b_recv.at[j, k], peer)
            for j, peer in enumerate(partners)
        ]

    def last(k):
        place = done.at[rows(mine + k * tile, tile)]
        return copy(place, place, c_send.at[k], c_recv.at[k], sibling)

    def enter():
        barrier = pltpu.get_barrier_semaphore()
        for peer in [sibling] + partners:
            pl.semaphore_signal(barrier, inc=1, device_id={"bus": peer}, device_id_type=MESH)
        pl.semaphore_wait(barrier, 1 + len(partners))

    def halve(k):
        first(k).wait_recv()
        begin = 2 * half if isinstance(k, int) and k == pairs else mine + k * tile
        here = rows(k * tile, size_of(k))
        chips[chip, here, :] = part[rows(begin, size_of(k)), :] + there[here, :]
        for each in cross(k):
            each.start()

    def total(k):
        for each in cross(k):
            each.wait_recv()
        here = rows(k * tile, size_of(k))
        value = chips[0, here, :]
        for c in range(1, chip_count):
            value = value + chips[c, here, :]
        return value

    def end():
        for k in range(pairs + 1):
            first(k).wait_send()
            for each in cross(k):
                each.wait_send()
        for k in range(pairs):
            last(k).wait_send()

    return enter, first, halve, total, last, end, rows, mine, other


def run_stages(steps, tile, make_tile, update, extra_ref, extra_out, part, there, chips, done, sems):
    enter, first, halve, total, last, end, rows, mine, other = stages(
        steps, tile, part, there, chips, done, sems
    )
    i = pl.program_id(0)
    pairs = steps // 2
    half = pairs * tile
    k = i // 2

    @pl.when(i == 0)
    def _():
        enter()
        part[2 * half:2 * half + 8, :] = extra_ref[...]
        first(pairs).start()

    part[rows((i % 2) * half + k * tile, tile), :] = make_tile()

    @pl.when(i == 1)
    def _():
        halve(pairs)

    @pl.when(i % 2 == 1)
    def _():
        first(k).start()

        @pl.when(k >= 1)
        def _():
            halve(k - 1)

    @pl.when(i == steps - 1)
    def _():
        halve(pairs - 1)
        for c in range(pairs):
            here = rows(mine + c * tile, tile)
            done[here, :] = total(c)
            last(c).start()
            update(here)
        extra_out[...] = total(pairs)
        for c in range(pairs):
            last(c).wait_recv()
            update(rows(other + c * tile, tile))
        end()


def store_dual_parts(moved, rating, here, dual_out, cat_out):
    hours = moved.shape[1]
    bound = DUAL_STEP * rating
    dual = moved - jnp.clip(moved, -bound, bound)
    high = dual.astype(jnp.bfloat16)
    dual_out[here, :] = dual
    cat_out[here, :hours] = high
    cat_out[here, hours:] = (dual - high.astype(jnp.float32)).astype(jnp.bfloat16)


def setup_kernel(
    groups, units, sub, steps, tile,
    ptdf_ref, pick_ref, load_ref, rating_ref, extra_ref,
    high_ref, low_ref, flow_out, dual_out, cat_out, extra_out,
    part, there, chips, done, *sems,
):
    hours = part.shape[1]

    def make_tile():
        flow = jnp.zeros((tile, hours), jnp.float32)
        for g in range(groups):
            block = ptdf_ref[:, g * sub:(g + 1) * sub]
            high = block.astype(jnp.bfloat16)
            low = (block - high.astype(jnp.float32)).astype(jnp.bfloat16)
            pick = pick_ref[g * sub:(g + 1) * sub, :]
            load = load_ref[g * sub:(g + 1) * sub, :]
            own = slice(g * units, (g + 1) * units)
            high_ref[:, own] = jnp.dot(
                high, pick, preferred_element_type=jnp.float32
            ).astype(jnp.bfloat16)
            low_ref[:, own] = jnp.dot(
                low, pick, preferred_element_type=jnp.float32
            ).astype(jnp.bfloat16)
            wide = jnp.dot(high, load, preferred_element_type=jnp.float32)
            flow += wide[:, :hours] + wide[:, hours:]
            flow += jnp.dot(low, load[:, :hours], preferred_element_type=jnp.float32)
        return flow

    def update(here):
        flow = done[here, :]
        flow_out[here, :] = flow
        store_dual_parts(DUAL_STEP * flow, rating_ref[here, :], here, dual_out, cat_out)

    run_stages(
        steps, tile, make_tile, update, extra_ref, extra_out, part, there, chips, done, sems
    )


def flow_kernel(
    steps, tile,
    high_ref, low_ref, change_ref, rating_ref, flow_ref, dual_ref, extra_ref,
    dual_out, cat_out, extra_out,
    part, there, chips, done, *sems,
):
    hours = part.shape[1]

    def make_tile():
        wide = jnp.dot(high_ref[...], change_ref[...], preferred_element_type=jnp.float32)
        narrow = jnp.dot(
            low_ref[...], change_ref[:, :hours], preferred_element_type=jnp.float32
        )
        return wide[:, :hours] + wide[:, hours:] + narrow

    def update(here):
        moved = dual_ref[here, :] + DUAL_STEP * (flow_ref[here, :] + done[here, :])
        store_dual_parts(moved, rating_ref[here, :], here, dual_out, cat_out)

    run_stages(
        steps, tile, make_tile, update, extra_ref, extra_out, part, there, chips, done, sems
    )


def tiles_of(lines):
    half = lines // 2
    sizes = (384, 320, 240, 192, 160, 128, 96, 64, 48, 32, 16)
    tile = next(t for t in sizes if half % t == 0)
    return 2 * (half // tile), tile


def whole(shape):
    return pl.BlockSpec(shape, lambda i: (0, 0), pipeline_mode=pl.Buffered(1))


def flow_scratch(lines, hours, steps):
    chip_count, pairs = lax.axis_size("bus") // 2, steps // 2
    first = pltpu.SemaphoreType.DMA((pairs + 1,))
    many = pltpu.SemaphoreType.DMA((chip_count - 1, pairs + 1))
    last = pltpu.SemaphoreType.DMA((pairs,))
    return [
        pltpu.VMEM((lines + 8, hours), jnp.float32),
        pltpu.VMEM((lines // 2 + 8, hours), jnp.float32),
        pltpu.VMEM((chip_count, lines // 2 + 8, hours), jnp.float32),
        pltpu.VMEM((lines, hours), jnp.float32),
        first, first, many, many, last, last,
    ]


def set_up(ptdf, pick, load, rating, extra, groups, units, sub):
    lines, buses = ptdf.shape
    hours = rating.shape[1]
    steps, tile = tiles_of(lines)
    chosen = groups * units
    pairs = steps // 2

    def order(i):
        return ((i % 2) * pairs + i // 2, 0)

    full = whole((lines, hours))
    return pl.pallas_call(
        functools.partial(setup_kernel, groups, units, sub, steps, tile),
        grid=(steps,),
        in_specs=[
            pl.BlockSpec((tile, buses), order),
            whole((buses, units)),
            whole((buses, 2 * hours)),
            full,
            whole((8, hours)),
        ],
        out_specs=[
            pl.BlockSpec((tile, chosen), order),
            pl.BlockSpec((tile, chosen), order),
            full,
            full,
            whole((lines, 2 * hours)),
            whole((8, hours)),
        ],
        out_shape=[
            jax.ShapeDtypeStruct((lines, chosen), jnp.bfloat16),
            jax.ShapeDtypeStruct((lines, chosen), jnp.bfloat16),
            jax.ShapeDtypeStruct((lines, hours), jnp.float32),
            jax.ShapeDtypeStruct((lines, hours), jnp.float32),
            jax.ShapeDtypeStruct((lines, 2 * hours), jnp.bfloat16),
            jax.ShapeDtypeStruct((8, hours), jnp.float32),
        ],
        scratch_shapes=flow_scratch(lines, hours, steps),
        compiler_params=pltpu.CompilerParams(
            collective_id=0, has_side_effects=True, vmem_limit_bytes=52 * 1024 * 1024
        ),
        cost_estimate=pl.CostEstimate(
            flops=4 * lines * buses * (units + 2 * hours),
            bytes_accessed=4 * lines * (buses + chosen + hours),
            transcendentals=0,
        ),
        name="first_flow",
    )(ptdf, pick, load, rating, extra)


def flow_step(high, low, change, rating, flow_first, dual, extra):
    lines, chosen = high.shape
    hours = dual.shape[1]
    steps, tile = tiles_of(lines)
    pairs = steps // 2

    def order(i):
        return ((i % 2) * pairs + i // 2, 0)

    full = whole((lines, hours))
    return pl.pallas_call(
        functools.partial(flow_kernel, steps, tile),
        grid=(steps,),
        in_specs=[
            pl.BlockSpec((tile, chosen), order),
            pl.BlockSpec((tile, chosen), order),
            whole((chosen, 2 * hours)),
            full,
            full,
            full,
            whole((8, hours)),
        ],
        out_specs=[full, whole((lines, 2 * hours)), whole((8, hours))],
        out_shape=[
            jax.ShapeDtypeStruct((lines, hours), jnp.float32),
            jax.ShapeDtypeStruct((lines, 2 * hours), jnp.bfloat16),
            jax.ShapeDtypeStruct((8, hours), jnp.float32),
        ],
        scratch_shapes=flow_scratch(lines, hours, steps),
        compiler_params=pltpu.CompilerParams(
            collective_id=4, has_side_effects=True, vmem_limit_bytes=44 * 1024 * 1024
        ),
        cost_estimate=pl.CostEstimate(
            flops=6 * lines * chosen * hours,
            bytes_accessed=4 * lines * (chosen + 6 * hours),
            transcendentals=0,
        ),
        name="flow_step",
    )(high, low, change, rating, flow_first, dual, extra)


def greet(axis):
    me, count = lax.axis_index(axis), lax.axis_size(axis)
    peers = [lax.rem(me + j, count) for j in range(1, count)]
    barrier = pltpu.get_barrier_semaphore()
    for peer in peers:
        pl.semaphore_signal(barrier, inc=1, device_id={axis: peer}, device_id_type=MESH)
    pl.semaphore_wait(barrier, count - 1)
    return me, peers


def gather_kernel(block_ref, out_ref, send_sem, recv_sem):
    me, peers = greet("line")
    own = out_ref.at[me]
    copies = [
        pltpu.make_async_remote_copy(
            src_ref=block_ref,
            dst_ref=own,
            send_sem=send_sem.at[j],
            recv_sem=recv_sem.at[j],
            device_id={"line": peer},
            device_id_type=MESH,
        )
        for j, peer in enumerate(peers)
    ]
    for copy in copies:
        copy.start()
    out_ref[me] = block_ref[...]
    for copy in copies:
        copy.wait_recv()
    for copy in copies:
        copy.wait_send()


def scatter_kernel(parts_ref, out_ref, slots, send_sem, recv_sem):
    me, peers = greet("line")
    copies = [
        pltpu.make_async_remote_copy(
            src_ref=parts_ref.at[peer],
            dst_ref=slots.at[j],
            send_sem=send_sem.at[j],
            recv_sem=recv_sem.at[j],
            device_id={"line": peer},
            device_id_type=MESH,
        )
        for j, peer in enumerate(peers)
    ]
    for copy in copies:
        copy.start()
    for copy in copies:
        copy.wait_recv()
    total = parts_ref[me]
    for j in range(len(peers)):
        total = total + slots[j]
    out_ref[...] = total
    for copy in copies:
        copy.wait_send()


def line_call(kernel, value, shape, slots, ident, name):
    sems = pltpu.SemaphoreType.DMA((lax.axis_size("line") - 1,))
    return pl.pallas_call(
        kernel,
        out_shape=jax.ShapeDtypeStruct(shape, value.dtype),
        in_specs=[pl.BlockSpec(memory_space=pltpu.VMEM)],
        out_specs=pl.BlockSpec(memory_space=pltpu.VMEM),
        scratch_shapes=slots + [sems, sems],
        compiler_params=pltpu.CompilerParams(
            collective_id=ident, has_side_effects=True, vmem_limit_bytes=32 * 1024 * 1024
        ),
        name=name,
    )(value)


def gather_line(value, ident):
    shape = (lax.axis_size("line"),) + value.shape
    return line_call(gather_kernel, value, shape, [], ident, "gather_line")


def scatter_line(value, ident):
    count = lax.axis_size("line")
    shape = (value.shape[0] // count,) + value.shape[1:]
    slots = [pltpu.VMEM((count - 1,) + shape, value.dtype)]
    return line_call(
        scatter_kernel, value.reshape((count,) + shape), shape, slots, ident, "scatter_line"
    )


def on_device(ptdf_matrix, bus_load, unit_bus, unit_type, unit_limit, unit_cost, line_rating):
    line_place = lax.axis_index("line")
    bus_place = lax.axis_index("bus")
    tm_place = lax.axis_index("tm")
    groups = lax.axis_size("line")
    lines, block_rows = ptdf_matrix.shape
    sub = block_rows // groups
    hour_dev = bus_load.shape[1]
    units = unit_bus.shape[0]
    cost, lower_limit, upper_limit, ramp, storage, energy = unit_tables(
        unit_type, unit_limit, unit_cost
    )
    first = jnp.clip(-PRIMAL_STEP * cost, lower_limit, upper_limit)
    extrap_first = 2.0 * first
    place = (unit_bus - bus_place * block_rows - line_place * sub).astype(jnp.float32)
    both = gather_line(jnp.stack([place, extrap_first] * 4), 1)
    places = both[:, 0].astype(jnp.int32)
    first_all = both[:, 1]
    pick = places[:, None, :] == jnp.arange(sub, dtype=jnp.int32)[None, :, None]
    placed = jnp.sum(jnp.where(pick, first_all[:, None, :], 0.0), axis=2).reshape(block_rows)
    pick = pick.astype(jnp.bfloat16).reshape(block_rows, units)
    injected = placed[:, None] - bus_load
    rating = jnp.broadcast_to(
        (line_rating.astype(jnp.float32) / 100.0)[:, None], (lines, hour_dev)
    )
    load_total = jnp.sum(bus_load, axis=0)

    def eight(surplus):
        return jnp.broadcast_to(surplus[None, :], (8, hour_dev))

    columns_high, columns_low, flow_first, line_dual, dual_cat, surplus = set_up(
        ptdf_matrix,
        pick,
        jnp.concatenate(parts(injected), axis=1),
        rating,
        eight(jnp.sum(first_all) - load_total),
        groups,
        units,
        sub,
    )
    earlier_index = jnp.arange(hour_dev, dtype=jnp.int32)[:, None]
    later_index = jnp.arange(hour_dev, dtype=jnp.int32)[None, :]
    forward_table = (earlier_index <= later_index).astype(jnp.float32)
    backward_table = (earlier_index >= later_index).astype(jnp.float32)
    hour_mask = (tm_place * hour_dev + jnp.arange(hour_dev, dtype=jnp.int32) >= 1).astype(
        jnp.float32
    )[None, :]
    generation = jnp.zeros((units, hour_dev), jnp.float32)
    ramp_dual = jnp.zeros((units, hour_dev), jnp.float32)
    store_dual = jnp.zeros((units, hour_dev), jnp.float32)
    balance_dual = jnp.zeros((hour_dev,), jnp.float32)
    for iteration in range(ITERS):
        if iteration == 0:
            updated = jnp.broadcast_to(first[:, None], (units, hour_dev))
            extrap = 2.0 * updated
            prev_edge = jnp.where(tm_place > 0, extrap_first, 0.0)
            store_before = extrap_first * (tm_place * hour_dev).astype(jnp.float32)
        else:
            over_lines = (((0,), (0,)), ((), ()))
            wide = lax.dot_general(
                columns_high,
                dual_cat,
                over_lines,
                preferred_element_type=jnp.float32,
            )
            narrow = lax.dot_general(
                columns_low, dual_cat[:, :hour_dev], over_lines, preferred_element_type=jnp.float32
            )
            unit_price = scatter_line(wide[:, :hour_dev] + wide[:, hour_dev:] + narrow, 3)
            ramp_edge, store_after = gathered(
                ramp_dual[:, 0], jnp.sum(store_dual, axis=1), "tm", -1
            )
            ramp_next = jnp.concatenate([ramp_dual[:, 1:], ramp_edge[:, None]], axis=1)
            suffix = exact(store_dual, backward_table) + store_after[:, None]
            gradient = (
                cost[:, None]
                + balance_dual[None, :]
                + unit_price
                + ramp_dual
                - ramp_next
                + storage[:, None] * suffix
            )
            updated = jnp.clip(
                generation - PRIMAL_STEP * gradient, lower_limit[:, None], upper_limit[:, None]
            )
            extrap = 2.0 * updated - generation
            extrap_all = gather_line(extrap, 2).reshape(-1, hour_dev)
            change = extrap_all - first_all.reshape(-1)[:, None]
            line_dual, dual_cat, surplus = flow_step(
                columns_high,
                columns_low,
                jnp.concatenate(parts(change), axis=1),
                rating,
                flow_first,
                line_dual,
                eight(jnp.sum(extrap_all, axis=0) - load_total),
            )
            prev_edge, store_before = gathered(extrap[:, -1], jnp.sum(extrap, axis=1), "tm", 1)
        if iteration == ITERS - 1:
            return (updated, line_dual)
        balance_dual = balance_dual + surplus[0] / UNITS
        previous = jnp.concatenate([prev_edge[:, None], extrap[:, :-1]], axis=1)
        moved = ramp_dual + DUAL_STEP * (extrap - previous) * hour_mask
        ramp_dual = moved - jnp.clip(moved, -DUAL_STEP * ramp[:, None], DUAL_STEP * ramp[:, None])
        running = exact(extrap, forward_table) + store_before[:, None]
        moved = store_dual + DUAL_STEP * storage[:, None] * running
        store_dual = moved - jnp.clip(
            moved, -DUAL_STEP * energy[:, None], DUAL_STEP * energy[:, None]
        )
        generation = updated


def solution(mesh):
    return jax.shard_map(
        on_device,
        mesh=mesh,
        in_specs=(
            P("line", "bus"),
            P("bus", "tm"),
            P(("line", "bus")),
            P(("line", "bus")),
            P(("line", "bus")),
            P(("line", "bus")),
            P("line"),
        ),
        out_specs=(P(("line", "bus"), "tm"), P("line", "tm")),
        check_vma=False,
    )
```

profile of v0, /device:TPU:0, one launch (start us, length us, event | category | flops | bytes accessed | tf_op | source)
XLA Modules:
  0.0 305.4 jit_solution(1467551710553482002)
XLA Ops:
  0.7 0.7 iota_compare_fusion.19
  1.4 0.8 select_reduce_fusion.1
  2.2 0.7 broadcast_multiply_fusion.1
  2.9 0.1 copy.16
  3.1 0.2 minimum_subtract_fusion.5
  3.5 0.4 fusion.41
  3.8 1.3 collective-permute-start
  5.1 0.7 subtract_convert_fusion
  5.9 7.4 %gather_line.4 = f32[4,8,256]{2,1,0:T(8,128)S(1)} custom-call(f32[8,256]{1,0:T(8,128)S(1)} %stack.47.block_ref), custom_call_target="tpu_custom_call" | custom-call | tf_op jit(solution)/shard_map/gather_line/pallas_call | solution.py:435
  13.3 0.6 slice_reduce_fusion.6
  13.9 0.5 select_reduce_fusion
  14.5 0.5 fusion.pick_ref
  15.0 0.9 copy-done.11
  15.9 0.5 reduce-precision_convert_fusion
  16.3 1.3 pad_maximum_fusion.load_ref
  17.7 0.6 broadcast_subtract_fusion
  18.3 1.8 broadcast_in_dim.36.rating_ref
  20.2 46.9 %first_flow.1 = (bf16[3840,1024]{1,0:T(8,128)(2,1)}, bf16[3840,1024]{1,0:T(8,128)(2,1)}, f32[3840,128]{1,0:T(8,128)}, f32[3840,128]{1,0:T(8,128)}, bf16[3840,256]{1,0:T(8,128)(2,1)}, /*index=5*/f32[8,128]{1,0:T(8,128)S(1)}) custom-call(f32[3840,3072]{1,0:T(8,128)} %ptdf_ref.1, bf16[3072,256]{1,0:T(8,128)(2,1)S(1)} %fusion.pick_ref, ...), custom_call_target="tpu_custom_call" | custom-call | flops 24159191040 | bytes 64880640 | tf_op jit(solution)/shard_map/first_flow/pallas_call | solution.py:295
  67.1 6.2 %fusion.44 = f32[1024,256]{1,0:T(8,128)S(1)} fusion(bf16[3840,1024]{1,0:T(8,128)(2,1)} %get-tuple-element.16.high_ref, bf16[3840,256]{1,0:T(8,128)(2,1)} %get-tuple-element.17), kind=kOutput, calls=%fused_computation.126 | convolution fusion | flops 2013265920 | bytes 10878976 | tf_op jit(solution)/shard_map/dot_general | solution.py:521
  73.3 0.4 copy-done.10
  73.7 2.4 convolution_add_fusion.2
  76.2 13.5 %scatter_line.3 = f32[256,128]{1,0:T(8,128)S(1)} custom-call(f32[4,256,128]{2,1,0:T(8,128)S(1)} %bitcast.86), custom_call_target="tpu_custom_call" | custom-call | tf_op jit(solution)/shard_map/scatter_line/pallas_call | solution.py:435
  89.7 0.1 copy.18
  89.9 0.4 fusion.37
  90.3 15.0 %gather_line.5 = f32[4,256,128]{2,1,0:T(8,128)S(1)} custom-call(f32[256,128]{1,0:T(8,128)S(1)} %get-tuple-element.33.block_ref), custom_call_target="tpu_custom_call" | custom-call | tf_op jit(solution)/shard_map/gather_line/pallas_call | solution.py:435
  105.3 0.2 slice_reduce_fusion.3
  105.5 0.2 reduce_sum.123
  105.7 0.2 reduce-precision_convert_fusion.3
  106.0 1.2 copy-done.1
  107.2 1.5 copy-done.8
  108.7 29.9 %flow_step.3 = (f32[3840,128]{1,0:T(8,128)S(1)}, bf16[3840,256]{1,0:T(8,128)(2,1)S(1)}, f32[8,128]{1,0:T(8,128)S(1)}) custom-call(bf16[3840,1024]{1,0:T(8,128)(2,1)} %get-tuple-element.16.high_ref, bf16[3840,1024]{1,0:T(8,128)(2,1)} %get-tuple-element.18.low_ref, bf16[1024,256]{1,0:T(8,128)(2,1)S(1)} %pad_maximum_fusion.1.change_ref, ...), custom_call_target="tpu_custom_call" | custom-call | flops 3019898880 | bytes 27525120 | tf_op jit(solution)/shard_map/flow_step/pallas_call | solution.py:344
  138.6 6.2 %fusion.45 = f32[1024,256]{1,0:T(8,128)S(1)} fusion(bf16[3840,1024]{1,0:T(8,128)(2,1)} %get-tuple-element.16.high_ref, bf16[3840,256]{1,0:T(8,128)(2,1)S(1)} %get-tuple-element.22), kind=kOutput, calls=%fused_computation.127 | convolution fusion | flops 2013265920 | bytes 10878976 | tf_op jit(solution)/shard_map/dot_general | solution.py:521
  144.8 4.6 %collective-permute-start.1 = (f32[2,256]{1,0:T(2,128)S(1)}, f32[2,256]{1,0:T(2,128)S(1)}, u32[]{:S(2)}, u32[]{:S(2)}) collective-permute-start(f32[2,256]{1,0:T(2,128)S(1)} %pad_maximum_fusion.5), channel_id=1, source_target_pairs={{0,1},{2,3},{4,5},{6,7},{8,9},{10,11},{12,13},{14,15},{16,17},{18,... | collective-permute-start | bytes 6152 | tf_op jit(solution)/shard_map/ppermute | solution.py:49
  149.4 5.6 %convolution_add_fusion.1 = f32[1024,128]{1,0:T(8,128)S(1)} fusion(bf16[3840,1024]{1,0:T(8,128)(2,1)} %get-tuple-element.18.low_ref, bf16[3840,256]{1,0:T(8,128)(2,1)S(1)} %get-tuple-element.22, f32[1024,256]{1,0:T(8,128)S(1)} %fusion.45), kind=kOutput, calls=%fused_computation.9 | convolution fusion | flops 1006895104 | bytes 10420224 | tf_op jit(solution)/shard_map/dot_general | solution.py:527
  155.0 0.1 copy.20
  155.1 0.2 minimum_subtract_fusion.3
  155.5 0.3 fusion.42
  155.8 1.3 collective-permute-start.2
  157.2 15.0 %scatter_line.4 = f32[256,128]{1,0:T(8,128)S(1)} custom-call(f32[4,256,128]{2,1,0:T(8,128)S(1)} %bitcast.85), custom_call_target="tpu_custom_call" | custom-call | tf_op jit(solution)/shard_map/scatter_line/pallas_call | solution.py:435
  172.3 0.1 copy.22
  172.5 0.4 fusion.36
  172.8 14.8 %gather_line.6 = f32[4,256,128]{2,1,0:T(8,128)S(1)} custom-call(f32[256,128]{1,0:T(8,128)S(1)} %get-tuple-element.31.block_ref), custom_call_target="tpu_custom_call" | custom-call | tf_op jit(solution)/shard_map/gather_line/pallas_call | solution.py:435
  187.6 0.2 reduce_sum.126
  187.8 0.2 reduce-precision_convert_fusion.2
  188.0 0.2 slice_reduce_fusion.1
  188.2 1.1 copy-done.2
  189.3 1.5 copy-done.7
  190.9 29.9 %flow_step.4 = (f32[3840,128]{1,0:T(8,128)S(1)}, bf16[3840,256]{1,0:T(8,128)(2,1)S(1)}, f32[8,128]{1,0:T(8,128)S(1)}) custom-call(bf16[3840,1024]{1,0:T(8,128)(2,1)} %get-tuple-element.16.high_ref, bf16[3840,1024]{1,0:T(8,128)(2,1)} %get-tuple-element.18.low_ref, bf16[1024,256]{1,0:T(8,128)(2,1)S(1)} %pad_maximum_fusion.2.change_ref, ...), custom_call_target="tpu_custom_call" | custom-call | flops 3019898880 | bytes 27525120 | tf_op jit(solution)/shard_map/flow_step/pallas_call | solution.py:344
  220.8 6.2 %fusion.46 = f32[1024,256]{1,0:T(8,128)S(1)} fusion(bf16[3840,1024]{1,0:T(8,128)(2,1)} %get-tuple-element.16.high_ref, bf16[3840,256]{1,0:T(8,128)(2,1)S(1)} %get-tuple-element.25), kind=kOutput, calls=%fused_computation.128 | convolution fusion | flops 2013265920 | bytes 10878976 | tf_op jit(solution)/shard_map/dot_general | solution.py:521
  226.9 4.6 %collective-permute-start.3 = (f32[2,256]{1,0:T(2,128)S(1)}, f32[2,256]{1,0:T(2,128)S(1)}, u32[]{:S(2)}, u32[]{:S(2)}) collective-permute-start(f32[2,256]{1,0:T(2,128)S(1)} %pad_maximum_fusion.7), channel_id=1, source_target_pairs={{0,1},{2,3},{4,5},{6,7},{8,9},{10,11},{12,13},{14,15},{16,17},{18,... | collective-permute-start | bytes 6152 | tf_op jit(solution)/shard_map/ppermute | solution.py:49
  231.5 5.6 %convolution_add_fusion = f32[1024,128]{1,0:T(8,128)S(1)} fusion(bf16[3840,1024]{1,0:T(8,128)(2,1)} %get-tuple-element.18.low_ref, bf16[3840,256]{1,0:T(8,128)(2,1)S(1)} %get-tuple-element.25, f32[1024,256]{1,0:T(8,128)S(1)} %fusion.46), kind=kOutput, calls=%fused_computation.8 | convolution fusion | flops 1006895104 | bytes 10420224 | tf_op jit(solution)/shard_map/dot_general | solution.py:527
  237.1 0.1 copy.24
  237.2 0.2 minimum_subtract_fusion.1
  237.5 0.3 fusion.43
  237.9 1.3 collective-permute-start.4
  239.2 14.5 %scatter_line.5 = f32[256,128]{1,0:T(8,128)S(1)} custom-call(f32[4,256,128]{2,1,0:T(8,128)S(1)} %bitcast.84), custom_call_target="tpu_custom_call" | custom-call | tf_op jit(solution)/shard_map/scatter_line/pallas_call | solution.py:435
  253.9 1.0 multiply_subtract_fusion
  254.9 14.8 %gather_line.7 = f32[4,256,128]{2,1,0:T(8,128)S(1)} custom-call(f32[256,128]{1,0:T(8,128)S(1)} %get-tuple-element.78.block_ref), custom_call_target="tpu_custom_call" | custom-call | tf_op jit(solution)/shard_map/gather_line/pallas_call | solution.py:435
  269.7 0.2 reduce_sum.129
  269.8 0.2 reduce-precision_convert_fusion.1
  270.1 1.2 copy-done.3
  271.4 1.5 copy-done.5
  272.9 31.2 %flow_step.5 = (f32[3840,128]{1,0:T(8,128)S(1)}, bf16[3840,256]{1,0:T(8,128)(2,1)}, f32[8,128]{1,0:T(8,128)}) custom-call(bf16[3840,1024]{1,0:T(8,128)(2,1)} %get-tuple-element.16.high_ref, bf16[3840,1024]{1,0:T(8,128)(2,1)} %get-tuple-element.18.low_ref, bf16[1024,256]{1,0:T(8,128)(2,1)S(1)} %pad_maximum_fusion.3.change_ref, f32[3840,128]{1,0:T(8,128)S(1)} %copy-done, ...), custom_call_target="tpu_custom_call" | custom-call | flops 3019898880 | bytes 27525120 | tf_op jit(solution)/shard_map/flow_step/pallas_call | solution.py:344
  304.1 1.3 copy.39
  (66 shorter events, 1.3 us)
Async XLA Ops:
  0.6 14.3 %copy-start.12 = (s32[3840]{0:T(1024)S(1)}, s32[3840]{0:T(1024)}, u32[]{:S(2)}) copy-start(s32[3840]{0:T(1024)} %param.15) | copy-start | bytes 46084
  3.8 85.8 %collective-permute-start = (f32[2,256]{1,0:T(2,128)S(1)}, f32[2,256]{1,0:T(2,128)S(1)}, u32[]{:S(2)}, u32[]{:S(2)}) collective-permute-start(f32[2,256]{1,0:T(2,128)S(1)} %pad_maximum_fusion.4), channel_id=1, source_target_pairs={{1,0},{3,2},{5,4},{7,6},{9,8},{11,10},{13,12},{15,14},{17,16},{19,... | collective-permute-start | bytes 6152 | tf_op jit(solution)/shard_map/ppermute | solution.py:49
  14.4 1.4 copy-start.11
  67.1 6.2 %copy-start.9 = (bf16[3840,1024]{1,0:T(8,128)(2,1)S(1)}, bf16[3840,1024]{1,0:T(8,128)(2,1)}, u32[]{:S(2)}) copy-start(bf16[3840,1024]{1,0:T(8,128)(2,1)} %get-tuple-element.18.low_ref) | copy-start | bytes 23592964
  67.1 6.6 %copy-start.10 = (bf16[3840,256]{1,0:T(8,128)(2,1)S(1)}, bf16[3840,256]{1,0:T(8,128)(2,1)}, u32[]{:S(2)}) copy-start(bf16[3840,256]{1,0:T(8,128)(2,1)} %get-tuple-element.17) | copy-start | bytes 5898244
  89.8 16.1 %copy-start = (f32[3840,128]{1,0:T(8,128)S(1)}, f32[3840,128]{1,0:T(8,128)}, u32[]{:S(2)}) copy-start(f32[3840,128]{1,0:T(8,128)} %broadcast_in_dim.36.rating_ref) | copy-start | bytes 5898244
  105.6 1.6 copy-start.1
  107.2 1.5 copy-start.8
  138.6 6.2 %copy-start.6 = (f32[3840,128]{1,0:T(8,128)}, f32[3840,128]{1,0:T(8,128)S(1)}, u32[]{:S(2)}) copy-start(f32[3840,128]{1,0:T(8,128)S(1)} %get-tuple-element.23.dual_ref) | copy-start | bytes 5898244
  144.8 10.2 %collective-permute-start.1 = (f32[2,256]{1,0:T(2,128)S(1)}, f32[2,256]{1,0:T(2,128)S(1)}, u32[]{:S(2)}, u32[]{:S(2)}) collective-permute-start(f32[2,256]{1,0:T(2,128)S(1)} %pad_maximum_fusion.5), channel_id=1, source_target_pairs={{0,1},{2,3},{4,5},{6,7},{8,9},{10,11},{12,13},{14,15},{16,17},{18,... | collective-permute-start | bytes 6152 | tf_op jit(solution)/shard_map/ppermute | solution.py:49
  155.8 16.4 %collective-permute-start.2 = (f32[2,256]{1,0:T(2,128)S(1)}, f32[2,256]{1,0:T(2,128)S(1)}, u32[]{:S(2)}, u32[]{:S(2)}) collective-permute-start(f32[2,256]{1,0:T(2,128)S(1)} %pad_maximum_fusion.6), channel_id=1, source_target_pairs={{1,0},{3,2},{5,4},{7,6},{9,8},{11,10},{13,12},{15,14},{17,16},{19,... | collective-permute-start | bytes 6152 | tf_op jit(solution)/shard_map/ppermute | solution.py:49
  187.8 1.5 copy-start.2
  189.3 1.5 copy-start.7
  220.7 6.2 %copy-start.4 = (f32[3840,128]{1,0:T(8,128)}, f32[3840,128]{1,0:T(8,128)S(1)}, u32[]{:S(2)}) copy-start(f32[3840,128]{1,0:T(8,128)S(1)} %get-tuple-element.26.dual_ref) | copy-start | bytes 5898244
  226.9 10.1 %collective-permute-start.3 = (f32[2,256]{1,0:T(2,128)S(1)}, f32[2,256]{1,0:T(2,128)S(1)}, u32[]{:S(2)}, u32[]{:S(2)}) collective-permute-start(f32[2,256]{1,0:T(2,128)S(1)} %pad_maximum_fusion.7), channel_id=1, source_target_pairs={{0,1},{2,3},{4,5},{6,7},{8,9},{10,11},{12,13},{14,15},{16,17},{18,... | collective-permute-start | bytes 6152 | tf_op jit(solution)/shard_map/ppermute | solution.py:49
  237.9 15.9 %collective-permute-start.4 = (f32[2,256]{1,0:T(2,128)S(1)}, f32[2,256]{1,0:T(2,128)S(1)}, u32[]{:S(2)}, u32[]{:S(2)}) collective-permute-start(f32[2,256]{1,0:T(2,128)S(1)} %pad_maximum_fusion.8), channel_id=1, source_target_pairs={{1,0},{3,2},{5,4},{7,6},{9,8},{11,10},{13,12},{15,14},{17,16},{19,... | collective-permute-start | bytes 6152 | tf_op jit(solution)/shard_map/ppermute | solution.py:49
  269.8 1.5 copy-start.3
  271.4 1.5 copy-start.5
where the time goes:
time: 308 us; the launch traced here: 305 us
  Pallas kernels  233 us (76%)
  matrix products  34.8 us (11%)
  local copies, waits for them, and re-layouts  14.6 us (5%)
  starting transfers between devices  13 us (4%)
  other arithmetic  8.88 us (3%)
    pallas_call x7, Pallas kernels, line_call(): pl.pallas_call(kernel, out_shape=jax.ShapeDtypeStruct(shape, value.dtype)...  95.1 us
    pallas_call x3, Pallas kernels, flow_step(): pl.pallas_call(functools.partial(flow_kernel, steps, tile), grid=(steps,)...  90.9 us
    pallas_call x1, Pallas kernels, set_up(): pl.pallas_call(functools.partial(setup_kernel, groups, units, sub, steps,...  46.9 us
    dot_general x3, matrix products, on_device(): lax.dot_general(columns_high, dual_cat, over_lines, preferred_element_typ...  18.5 us
    dot_general x3, matrix products, on_device(): lax.dot_general(columns_low, dual_cat[:, :hour_dev], over_lines, preferre...  13.5 us
    ppermute x5, starting transfers between devices, shifted(): return lax.ppermute(value, axis, pairs)  13 us
    unnamed x29, local copies, waits for them, and re-layouts  10.8 us
  transfers between devices with their start and end apart: 5, of which 0 were waited for; matrix products, arithmetic and copies ran while one was open for 9% of the time, Pallas kernels for 32%

commit v1 on v0

--- a/solution.py
+++ b/solution.py
@@ -43,23 +43,6 @@
     return jnp.dot(left, right, precision=lax.Precision.HIGHEST, preferred_element_type=jnp.float32)
 
 
-def shifted(value, axis, by):
-    length = lax.axis_size(axis)
-    pairs = [(i, i + by) for i in range(length) if 0 <= i + by < length]
-    return lax.ppermute(value, axis, pairs)
-
-
-def gathered(edge, total, axis, sign):
-    edge_there, total_there = jnp.zeros_like(edge), jnp.zeros_like(total)
-    for k in range(1, lax.axis_size(axis)):
-        if k == 1:
-            both = shifted(jnp.stack([edge, total]), axis, sign)
-            edge_there, total_there = both[0], both[1]
-        else:
-            total_there = total_there + shifted(total, axis, sign * k)
-    return edge_there, total_there
-
-
 def stages(steps, tile, part, there, chips, done, sems):
     a_send, a_recv, b_send, b_recv, c_send, c_recv = sems
     bus = lax.axis_index("bus")
@@ -210,11 +193,10 @@
             low = (block - high.astype(jnp.float32)).astype(jnp.bfloat16)
             pick = pick_ref[g * sub:(g + 1) * sub, :]
             load = load_ref[g * sub:(g + 1) * sub, :]
-            own = slice(g * units, (g + 1) * units)
-            high_ref[:, own] = jnp.dot(
+            high_ref[g] = jnp.dot(
                 high, pick, preferred_element_type=jnp.float32
             ).astype(jnp.bfloat16)
-            low_ref[:, own] = jnp.dot(
+            low_ref[g] = jnp.dot(
                 low, pick, preferred_element_type=jnp.float32
             ).astype(jnp.bfloat16)
             wide = jnp.dot(high, load, preferred_element_type=jnp.float32)
@@ -241,11 +223,14 @@
     hours = part.shape[1]
 
     def make_tile():
-        wide = jnp.dot(high_ref[...], change_ref[...], preferred_element_type=jnp.float32)
-        narrow = jnp.dot(
-            low_ref[...], change_ref[:, :hours], preferred_element_type=jnp.float32
-        )
-        return wide[:, :hours] + wide[:, hours:] + narrow
+        flow = jnp.zeros((tile, hours), jnp.float32)
+        for g in range(high_ref.shape[0]):
+            wide = jnp.dot(high_ref[g], change_ref[g], preferred_element_type=jnp.float32)
+            flow += wide[:, :hours] + wide[:, hours:]
+            flow += jnp.dot(
+                low_ref[g], change_ref[g, :, :hours], preferred_element_type=jnp.float32
+            )
+        return flow
 
     def update(here):
         moved = dual_ref[here, :] + DUAL_STEP * (flow_ref[here, :] + done[here, :])
@@ -264,7 +249,7 @@
 
 
 def whole(shape):
-    return pl.BlockSpec(shape, lambda i: (0, 0), pipeline_mode=pl.Buffered(1))
+    return pl.BlockSpec(shape, lambda i: (0,) * len(shape), pipeline_mode=pl.Buffered(1))
 
 
 def flow_scratch(lines, hours, steps):
@@ -291,6 +276,9 @@
     def order(i):
         return ((i % 2) * pairs + i // 2, 0)
 
+    def grouped(i):
+        return (0, (i % 2) * pairs + i // 2, 0)
+
     full = whole((lines, hours))
     return pl.pallas_call(
         functools.partial(setup_kernel, groups, units, sub, steps, tile),
@@ -303,16 +291,16 @@
             whole((8, hours)),
         ],
         out_specs=[
-            pl.BlockSpec((tile, chosen), order),
-            pl.BlockSpec((tile, chosen), order),
+            pl.BlockSpec((groups, tile, units), grouped),
+            pl.BlockSpec((groups, tile, units), grouped),
             full,
             full,
             whole((lines, 2 * hours)),
             whole((8, hours)),
         ],
         out_shape=[
-            jax.ShapeDtypeStruct((lines, chosen), jnp.bfloat16),
-            jax.ShapeDtypeStruct((lines, chosen), jnp.bfloat16),
+            jax.ShapeDtypeStruct((groups, lines, units), jnp.bfloat16),
+            jax.ShapeDtypeStruct((groups, lines, units), jnp.bfloat16),
             jax.ShapeDtypeStruct((lines, hours), jnp.float32),
             jax.ShapeDtypeStruct((lines, hours), jnp.float32),
             jax.ShapeDtypeStruct((lines, 2 * hours), jnp.bfloat16),
@@ -332,22 +320,23 @@
 
 
 def flow_step(high, low, change, rating, flow_first, dual, extra):
-    lines, chosen = high.shape
+    groups, lines, units = high.shape
+    chosen = groups * units
     hours = dual.shape[1]
     steps, tile = tiles_of(lines)
     pairs = steps // 2
 
-    def order(i):
-        return ((i % 2) * pairs + i // 2, 0)
+    def grouped(i):
+        return (0, (i % 2) * pairs + i // 2, 0)
 
     full = whole((lines, hours))
     return pl.pallas_call(
         functools.partial(flow_kernel, steps, tile),
         grid=(steps,),
         in_specs=[
-            pl.BlockSpec((tile, chosen), order),
-            pl.BlockSpec((tile, chosen), order),
-            whole((chosen, 2 * hours)),
+            pl.BlockSpec((groups, tile, units), grouped),
+            pl.BlockSpec((groups, tile, units), grouped),
+            whole((groups, units, 2 * hours)),
             full,
             full,
             full,
@@ -405,29 +394,154 @@
         copy.wait_send()
 
 
-def scatter_kernel(parts_ref, out_ref, slots, send_sem, recv_sem):
-    me, peers = greet("line")
-    copies = [
-        pltpu.make_async_remote_copy(
-            src_ref=parts_ref.at[peer],
-            dst_ref=slots.at[j],
-            send_sem=send_sem.at[j],
-            recv_sem=recv_sem.at[j],
-            device_id={"line": peer},
+def unit_kernel(
+    high_ref, low_ref, cat_ref, base_ref, info_ref, generation_ref, constant_ref,
+    updated_out, extrap_out, change_out, earlier_out, surplus_out,
+    high, low, flat, pieces, slots, later, own, everyone, earlier,
+    load_sem, price_send, price_recv, later_send, later_recv,
+    change_send, change_recv, earlier_send, earlier_recv,
+):
+    hours = base_ref.shape[1]
+    me, count = lax.axis_index("line"), lax.axis_size("line")
+    now, spans = lax.axis_index("tm"), lax.axis_size("tm")
+    peers = [lax.rem(me + j, count) for j in range(1, count)] + [me]
+    sides = [lax.rem(now + j, spans) for j in range(1, spans)]
+    loads = []
+    for j, peer in enumerate(peers):
+        loads.append(pltpu.make_async_copy(high_ref.at[peer], high.at[j], load_sem.at[0, j]))
+        loads.append(pltpu.make_async_copy(low_ref.at[peer], low.at[j], load_sem.at[1, j]))
+    for load in loads:
+        load.start()
+
+    barrier = pltpu.get_barrier_semaphore()
+    for peer in peers[:-1]:
+        pl.semaphore_signal(barrier, inc=1, device_id={"line": peer}, device_id_type=MESH)
+    for side in sides:
+        pl.semaphore_signal(barrier, inc=1, device_id={"tm": side}, device_id_type=MESH)
+    pl.semaphore_wait(barrier, count - 1 + spans - 1)
+
+    def send(source, target, send_sem, recv_sem, where):
+        copy = pltpu.make_async_remote_copy(
+            src_ref=source,
+            dst_ref=target,
+            send_sem=send_sem,
+            recv_sem=recv_sem,
+            device_id=where,
             device_id_type=MESH,
         )
-        for j, peer in enumerate(peers)
+        copy.start()
+        return copy
+
+    own[0] = info_ref[...]
+    hour_copies = [
+        send(own.at[0], later.at[j], later_send.at[j], later_recv.at[j], {"tm": side})
+        for j, side in enumerate(sides)
     ]
-    for copy in copies:
-        copy.start()
-    for copy in copies:
+    flat[...] = cat_ref[...].T
+    price_copies = []
+    for j, peer in enumerate(peers):
+        loads[2 * j].wait()
+        loads[2 * j + 1].wait()
+        wide = jnp.dot(flat[...], high[j], preferred_element_type=jnp.float32)
+        narrow = jnp.dot(flat[:hours, :], low[j], preferred_element_type=jnp.float32)
+        pieces[j] = (wide[:hours] + wide[hours:] + narrow).T
+        if j < count - 1:
+            price_copies.append(
+                send(pieces.at[j], slots.at[j], price_send.at[j], price_recv.at[j], {"line": peer})
+            )
+    info = info_ref[...]
+    gradient = base_ref[...]
+    for copy in hour_copies:
         copy.wait_recv()
-    total = parts_ref[me]
-    for j in range(len(peers)):
-        total = total + slots[j]
-    out_ref[...] = total
-    for copy in copies:
+    lane = lax.broadcasted_iota(jnp.int32, gradient.shape, 1)
+    store_after = jnp.zeros_like(info[:, 1:2])
+    for j in range(len(sides)):
+        source = lax.rem(now - (j + 1) + spans, spans)
+        there = later[j]
+        after = jnp.where(source > now, 1.0, 0.0)
+        beside = jnp.where(source == now + 1, 1.0, 0.0)
+        store_after = store_after + after * there[:, 1:2]
+        gradient = gradient - jnp.where(lane == hours - 1, beside * there[:, 0:1], 0.0)
+    gradient = gradient + info[:, 2:3] * store_after + pieces[count - 1]
+    for j, copy in enumerate(price_copies):
+        copy.wait_recv()
+        gradient = gradient + slots[j]
+    generation = generation_ref[...]
+    updated = jnp.clip(generation - PRIMAL_STEP * gradient, info[:, 3:4], info[:, 4:5])
+    extrap = 2.0 * updated - generation
+    own[1] = extrap
+    everyone[me] = extrap - info[:, 5:6]
+    place = everyone.at[me]
+    change_copies = [
+        send(place, place, change_send.at[j], change_recv.at[j], {"line": peer})
+        for j, peer in enumerate(peers[:-1])
+    ]
+    extrap_copies = [
+        send(own.at[1], earlier.at[j], earlier_send.at[j], earlier_recv.at[j], {"tm": side})
+        for j, side in enumerate(sides)
+    ]
+    updated_out[...] = updated
+    extrap_out[...] = extrap
+    for j, copy in enumerate(extrap_copies):
+        copy.wait_recv()
+        earlier_out[j] = earlier[j]
+    for copy in change_copies:
+        copy.wait_recv()
+    surplus = constant_ref[...]
+    for g in range(count):
+        change = everyone[g]
+        part = change.astype(jnp.bfloat16)
+        change_out[g, :, :hours] = part
+        change_out[g, :, hours:] = (change - part.astype(jnp.float32)).astype(jnp.bfloat16)
+        surplus = surplus + jnp.sum(change, axis=0, keepdims=True)
+    surplus_out[...] = surplus
+    for copy in hour_copies + price_copies + change_copies + extrap_copies:
         copy.wait_send()
+
+
+def unit_step(high, low, cat, base, info, generation, constant):
+    groups, lines, units = high.shape
+    hours = base.shape[1]
+    sides = lax.axis_size("tm") - 1
+    block = (units, hours)
+    line_sem = pltpu.SemaphoreType.DMA((groups - 1,))
+    tm_sem = pltpu.SemaphoreType.DMA((sides,))
+    near = pl.BlockSpec(memory_space=pltpu.VMEM)
+    far = pl.BlockSpec(memory_space=pl.ANY)
+    return pl.pallas_call(
+        unit_kernel,
+        in_specs=[far, far] + [near] * 5,
+        out_specs=[near] * 5,
+        out_shape=[
+            jax.ShapeDtypeStruct(block, jnp.float32),
+            jax.ShapeDtypeStruct(block, jnp.float32),
+            jax.ShapeDtypeStruct((groups, units, 2 * hours), jnp.bfloat16),
+            jax.ShapeDtypeStruct((sides,) + block, jnp.float32),
+            jax.ShapeDtypeStruct((8, hours), jnp.float32),
+        ],
+        scratch_shapes=[
+            pltpu.VMEM((groups, lines, units), jnp.bfloat16),
+            pltpu.VMEM((groups, lines, units), jnp.bfloat16),
+            pltpu.VMEM((2 * hours, lines), jnp.bfloat16),
+            pltpu.VMEM((groups,) + block, jnp.float32),
+            pltpu.VMEM((groups - 1,) + block, jnp.float32),
+            pltpu.VMEM((sides,) + block, jnp.float32),
+            pltpu.VMEM((2,) + block, jnp.float32),
+            pltpu.VMEM((groups,) + block, jnp.float32),
+            pltpu.VMEM((sides,) + block, jnp.float32),
+            pltpu.SemaphoreType.DMA((2, groups)),
+            line_sem, line_sem, tm_sem, tm_sem, line_sem, line_sem, tm_sem, tm_sem,
+        ],
+        compiler_params=pltpu.CompilerParams(
+            collective_id=3, has_side_effects=True, vmem_limit_bytes=44 * 1024 * 1024
+        ),
+        cost_estimate=pl.CostEstimate(
+            flops=6 * groups * lines * units * hours,
+            bytes_accessed=4 * groups * lines * units,
+            transcendentals=0,
+        ),
+        name="unit_step",
+    )(high, low, cat, base, info, generation, constant)
 
 
 def line_call(kernel, value, shape, slots, ident, name):
@@ -448,15 +562,6 @@
 def gather_line(value, ident):
     shape = (lax.axis_size("line"),) + value.shape
     return line_call(gather_kernel, value, shape, [], ident, "gather_line")
-
-
-def scatter_line(value, ident):
-    count = lax.axis_size("line")
-    shape = (value.shape[0] // count,) + value.shape[1:]
-    slots = [pltpu.VMEM((count - 1,) + shape, value.dtype)]
-    return line_call(
-        scatter_kernel, value.reshape((count,) + shape), shape, slots, ident, "scatter_line"
-    )
 
 
 def on_device(ptdf_matrix, bus_load, unit_bus, unit_type, unit_limit, unit_cost, line_rating):
@@ -489,12 +594,13 @@
     def eight(surplus):
         return jnp.broadcast_to(surplus[None, :], (8, hour_dev))
 
+    constant = eight(jnp.sum(first_all) - load_total)
     columns_high, columns_low, flow_first, line_dual, dual_cat, surplus = set_up(
         ptdf_matrix,
         pick,
         jnp.concatenate(parts(injected), axis=1),
         rating,
-        eight(jnp.sum(first_all) - load_total),
+        constant,
         groups,
         units,
         sub,
@@ -517,46 +623,30 @@
             prev_edge = jnp.where(tm_place > 0, extrap_first, 0.0)
             store_before = extrap_first * (tm_place * hour_dev).astype(jnp.float32)
         else:
-            over_lines = (((0,), (0,)), ((), ()))
-            wide = lax.dot_general(
-                columns_high,
-                dual_cat,
-                over_lines,
-                preferred_element_type=jnp.float32,
-            )
-            narrow = lax.dot_general(
-                columns_low, dual_cat[:, :hour_dev], over_lines, preferred_element_type=jnp.float32
-            )
-            unit_price = scatter_line(wide[:, :hour_dev] + wide[:, hour_dev:] + narrow, 3)
-            ramp_edge, store_after = gathered(
-                ramp_dual[:, 0], jnp.sum(store_dual, axis=1), "tm", -1
-            )
-            ramp_next = jnp.concatenate([ramp_dual[:, 1:], ramp_edge[:, None]], axis=1)
-            suffix = exact(store_dual, backward_table) + store_after[:, None]
-            gradient = (
+            ramp_next = jnp.pad(ramp_dual[:, 1:], ((0, 0), (0, 1)))
+            suffix = exact(store_dual, backward_table)
+            base = (
                 cost[:, None]
                 + balance_dual[None, :]
-                + unit_price
                 + ramp_dual
                 - ramp_next
                 + storage[:, None] * suffix
             )
-            updated = jnp.clip(
-                generation - PRIMAL_STEP * gradient, lower_limit[:, None], upper_limit[:, None]
+            head = [ramp_dual[:, 0], jnp.sum(store_dual, axis=1), storage]
+            tail = [lower_limit, upper_limit, extrap_first]
+            info = jnp.pad(jnp.stack(head + tail, axis=1), ((0, 0), (0, hour_dev - 6)))
+            updated, extrap, change, there, extra = unit_step(
+                columns_high, columns_low, dual_cat, base, info, generation, constant
             )
-            extrap = 2.0 * updated - generation
-            extrap_all = gather_line(extrap, 2).reshape(-1, hour_dev)
-            change = extrap_all - first_all.reshape(-1)[:, None]
             line_dual, dual_cat, surplus = flow_step(
-                columns_high,
-                columns_low,
-                jnp.concatenate(parts(change), axis=1),
-                rating,
-                flow_first,
-                line_dual,
-                eight(jnp.sum(extrap_all, axis=0) - load_total),
+                columns_high, columns_low, change, rating, flow_first, line_dual, extra
             )
-            prev_edge, store_before = gathered(extrap[:, -1], jnp.sum(extrap, axis=1), "tm", 1)
+            prev_edge, store_before = jnp.zeros_like(cost), jnp.zeros_like(cost)
+            for j in range(there.shape[0]):
+                span_count = lax.axis_size("tm")
+                source = (tm_place - (j + 1) + span_count) % span_count
+                prev_edge += jnp.where(source == tm_place - 1, there[j, :, -1], 0.0)
+                store_before += jnp.where(source < tm_place, jnp.sum(there[j], axis=1), 0.0)
         if iteration == ITERS - 1:
             return (updated, line_dual)
         balance_dual = balance_dual + surplus[0] / UNITS

time: 308 us -> 274 us (0.89)
  matrix products: 34.8 us -> 3.6 us
  starting transfers between devices: 13 us -> 0 us
  Pallas kernels: 233 us -> 239 us
    pallas_call x0 -> x3, Pallas kernels: none -> 93.9 us  [unit_step(): pl.pallas_call(unit_kernel, in_specs=[far, far] + [near] * 5, out_specs=[...]
    pallas_call x7 -> x1, Pallas kernels: 95.1 us -> 7.43 us  [line_call(): pl.pallas_call(kernel, out_shape=jax.ShapeDtypeStruct(shape, value.dtype)...]
    dot_general x6 -> x0, matrix products: 32 us -> none  [the longest x3 18.5 us: on_device(): lax.dot_general(columns_high, dual_cat, over_lines, preferred_element_typ...]
    ppermute x5 -> x0, starting transfers between devices: 13 us -> none  [shifted(): return lax.ppermute(value, axis, pairs)]
    unnamed x29 -> x66, local copies, waits for them, and re-layouts: 10.8 us -> 8.96 us
  transfers between devices with their start and end apart: 5 -> 0, of which waited for: 0 -> 0; matrix products, arithmetic and copies ran while one was open for 9% -> 0% of each run, Pallas kernels for 32% -> 0%
where the time goes in v1:
time: 274 us; the launch traced here: 270 us
  Pallas kernels  239 us (87%)
  local copies, waits for them, and re-layouts  14.9 us (5%)
  other arithmetic  11.1 us (4%)
  matrix products  3.6 us (1%)
    pallas_call x3, Pallas kernels, unit_step(): pl.pallas_call(unit_kernel, in_specs=[far, far] + [near] * 5, out_specs=[...  93.9 us
    pallas_call x3, Pallas kernels, flow_step(): pl.pallas_call(functools.partial(flow_kernel, steps, tile), grid=(steps,)...  91.3 us
    pallas_call x1, Pallas kernels, set_up(): pl.pallas_call(functools.partial(setup_kernel, groups, units, sub, steps,...  46.9 us
    unnamed x66, local copies, waits for them, and re-layouts  8.96 us
    pallas_call x1, Pallas kernels, line_call(): pl.pallas_call(kernel, out_shape=jax.ShapeDtypeStruct(shape, value.dtype)...  7.43 us

profile of v1, /device:TPU:0, one launch (start us, length us, event | category | flops | bytes accessed | tf_op | source)
XLA Modules:
  0.0 270.5 jit_solution(7072510062388066853)
XLA Ops:
  0.6 0.8 iota_compare_fusion.1
  1.4 0.2 select_reduce_fusion.1
  1.7 0.9 select_reduce_fusion.2
  2.6 0.7 broadcast_multiply_fusion.1
  3.4 0.7 subtract_convert_fusion
  4.1 7.4 %gather_line.1 = f32[4,8,256]{2,1,0:T(8,128)S(1)} custom-call(f32[8,256]{1,0:T(8,128)S(1)} %stack.50.block_ref), custom_call_target="tpu_custom_call" | custom-call | tf_op jit(solution)/shard_map/gather_line/pallas_call | solution.py:549
  11.5 0.6 slice_reduce_fusion
  12.1 0.5 select_reduce_fusion
  12.6 1.9 reduce-precision_convert_fusion
  14.5 0.0 copy-start.24
  14.5 1.4 pad_maximum_fusion.load_ref
  15.9 0.6 broadcast_subtract_fusion
  16.6 0.5 fusion.pick_ref
  17.1 1.8 broadcast_in_dim.37.rating_ref
  18.9 46.9 %first_flow.1 = (bf16[4,3840,256]{2,1,0:T(8,128)(2,1)}, bf16[4,3840,256]{2,1,0:T(8,128)(2,1)}, f32[3840,128]{1,0:T(8,128)}, f32[3840,128]{1,0:T(8,128)}, bf16[38...) custom-call(f32[3840,3072]{1,0:T(8,128)} %ptdf_ref.1, bf16[3072,256]{1,0:T(8,128)(2,1)S(1)} %fusion.pick_ref, ...), custom_call_target="tpu_custom_call" | custom-call | flops 24159191040 | bytes 64880640 | tf_op jit(solution)/shard_map/first_flow/pallas_call | solution.py:283
  65.9 0.0 copy-start.7
  65.9 0.1 slice.59
  66.0 0.0 copy-start.10
  66.0 0.1 copy.31
  66.2 0.0 copy-done.20
  66.2 0.2 minimum_subtract_fusion.5
  66.4 0.1 slice.73
  66.5 0.3 fusion.18
  66.9 0.3 fusion.3.base_ref
  67.2 0.1 copy.32
  67.3 0.1 copy.35
  67.5 0.1 copy.34
  67.7 0.1 copy.33
  67.8 0.1 slice_convert_fusion
  67.9 0.3 stack.55
  68.2 0.3 copy-done.8
  68.6 0.1 broadcast_in_dim.42.generation_ref
  68.7 28.6 %unit_step.3 = (f32[256,128]{1,0:T(8,128)S(1)}, f32[256,128]{1,0:T(8,128)S(1)}, bf16[4,256,256]{2,1,0:T(8,128)(2,1)S(1)}, f32[1,256,128]{2,1,0:T(8,128)S(1)}, f32[8,128]{1,0:T(8,128)S(1)}) custom-call(bf16[4,3840,256]{2,1,0:T(8,128)(2,1)} %get-tuple-element.28.high_ref, bf16[4,3840,256]{2,1,0:T(8,128)(2,1)} %get-tuple-element.29.low_ref, ...), custom_call_target="tpu_custom_call" | custom-call | flops 3019898880 | bytes 15728640 | tf_op jit(solution)/shard_map/unit_step/pallas_call | solution.py:511
  97.2 0.0 copy-start
  97.3 0.1 select_bitcast_fusion.1
  97.4 1.3 minimum_subtract_fusion.3
  98.7 0.1 reduce_sum.96
  98.9 1.2 fusion.19
  100.1 0.0 copy-start.9
  100.1 0.1 copy.36
  100.2 1.2 stack.57
  101.4 1.5 copy-done.1
  103.0 1.5 copy-done.4
  104.5 30.0 %flow_step.3 = (f32[3840,128]{1,0:T(8,128)S(1)}, bf16[3840,256]{1,0:T(8,128)(2,1)S(1)}, f32[8,128]{1,0:T(8,128)S(1)}) custom-call(bf16[4,3840,256]{2,1,0:T(8,128)(2,1)} %get-tuple-element.28.high_ref, bf16[4,3840,256]{2,1,0:T(8,128)(2,1)} %get-tuple-element.29.low_ref, bf16[4,256,256]{2,1,0:T(8,128)(2,1)S(1)} %get-tuple-element.32.change_ref, ...), custom_call_target="tpu_custom_call" | custom-call | flops 3019898880 | bytes 27525120 | tf_op jit(solution)/shard_map/flow_step/pallas_call | solution.py:333
  134.5 0.0 copy-start.5
  134.5 0.1 slice.75
  134.7 0.3 fusion.6.base_ref
  135.0 0.4 copy-done.29
  135.4 32.2 %unit_step.4 = (f32[256,128]{1,0:T(8,128)S(1)}, f32[256,128]{1,0:T(8,128)S(1)}, bf16[4,256,256]{2,1,0:T(8,128)(2,1)S(1)}, f32[1,256,128]{2,1,0:T(8,128)S(1)}, f32[8,128]{1,0:T(8,128)S(1)}) custom-call(bf16[4,3840,256]{2,1,0:T(8,128)(2,1)} %get-tuple-element.28.high_ref, bf16[4,3840,256]{2,1,0:T(8,128)(2,1)} %get-tuple-element.29.low_ref, ...), custom_call_target="tpu_custom_call" | custom-call | flops 3019898880 | bytes 15728640 | tf_op jit(solution)/shard_map/unit_step/pallas_call | solution.py:511
  167.6 0.1 select_bitcast_fusion
  167.8 0.2 minimum_subtract_fusion.1
  168.0 0.1 reduce_sum.98
  168.1 1.2 fusion.20
  169.3 0.1 copy.40
  169.4 1.2 stack.59
  170.6 1.5 copy-done.2
  172.2 1.5 copy-done.6
  173.7 30.0 %flow_step.4 = (f32[3840,128]{1,0:T(8,128)S(1)}, bf16[3840,256]{1,0:T(8,128)(2,1)S(1)}, f32[8,128]{1,0:T(8,128)S(1)}) custom-call(bf16[4,3840,256]{2,1,0:T(8,128)(2,1)} %get-tuple-element.28.high_ref, bf16[4,3840,256]{2,1,0:T(8,128)(2,1)} %get-tuple-element.29.low_ref, bf16[4,256,256]{2,1,0:T(8,128)(2,1)S(1)} %get-tuple-element.41.change_ref, ...), custom_call_target="tpu_custom_call" | custom-call | flops 3019898880 | bytes 27525120 | tf_op jit(solution)/shard_map/flow_step/pallas_call | solution.py:333
  203.7 0.1 slice.77
  203.8 0.3 fusion.9.base_ref
  204.2 33.1 %unit_step.5 = (f32[256,128]{1,0:T(8,128)S(1)}, f32[256,128]{1,0:T(8,128)}, bf16[4,256,256]{2,1,0:T(8,128)(2,1)S(1)}, f32[1,256,128]{2,1,0:T(8,128)}, f32[8,128]{1,0:T(8,128)S(1)}) custom-call(bf16[4,3840,256]{2,1,0:T(8,128)(2,1)} %get-tuple-element.28.high_ref, bf16[4,3840,256]{2,1,0:T(8,128)(2,1)} %get-tuple-element.29.low_ref, ...), custom_call_target="tpu_custom_call" | custom-call | flops 3019898880 | bytes 15728640 | tf_op jit(solution)/shard_map/unit_step/pallas_call | solution.py:511
  237.2 31.3 %flow_step.5 = (f32[3840,128]{1,0:T(8,128)S(1)}, bf16[3840,256]{1,0:T(8,128)(2,1)}, f32[8,128]{1,0:T(8,128)}) custom-call(bf16[4,3840,256]{2,1,0:T(8,128)(2,1)} %get-tuple-element.28.high_ref, bf16[4,3840,256]{2,1,0:T(8,128)(2,1)} %get-tuple-element.29.low_ref, bf16[4,256,256]{2,1,0:T(8,128)(2,1)S(1)} %get-tuple-element.50.change_ref, ...), custom_call_target="tpu_custom_call" | custom-call | flops 3019898880 | bytes 27525120 | tf_op jit(solution)/shard_map/flow_step/pallas_call | solution.py:333
  268.5 0.7 copy.52
  269.2 1.3 copy.53
  (67 shorter events, 0.2 us)
Async XLA Ops:
  1.7 64.9 %copy-start.25 = (f32[256]{0:T(256)}, f32[256]{0:T(256)S(1)}, u32[]{:S(2)}) copy-start(f32[256]{0:T(256)S(1)} %get-tuple-element.54) | copy-start | bytes 3076
  1.7 65.2 %copy-start.13 = (f32[256]{0:T(256)}, f32[256]{0:T(256)S(1)}, u32[]{:S(2)}) copy-start(f32[256]{0:T(256)S(1)} %get-tuple-element.55) | copy-start | bytes 3076
  3.3 62.9 %copy-start.20 = (f32[256]{0:T(256)}, f32[256]{0:T(256)S(1)}, u32[]{:S(2)}) copy-start(f32[256]{0:T(256)S(1)} %get-tuple-element.68) | copy-start | bytes 3076
  3.3 62.9 %copy-start.22 = (f32[256]{0:T(256)}, f32[256]{0:T(256)S(1)}, u32[]{:S(2)}) copy-start(f32[256]{0:T(256)S(1)} %get-tuple-element.69) | copy-start | bytes 3076
  3.3 63.2 %copy-start.26 = (f32[256]{0:T(256)}, f32[256]{0:T(256)S(1)}, u32[]{:S(2)}) copy-start(f32[256]{0:T(256)S(1)} %get-tuple-element.74) | copy-start | bytes 3076
  3.3 63.6 %copy-start.15 = (f32[256]{0:T(256)}, f32[256]{0:T(256)S(1)}, u32[]{:S(2)}) copy-start(f32[256]{0:T(256)S(1)} %get-tuple-element.73) | copy-start | bytes 3076
  3.3 64.2 %copy-start.18 = (f32[256]{0:T(256)}, f32[256]{0:T(256)S(1)}, u32[]{:S(2)}) copy-start(f32[256]{0:T(256)S(1)} %get-tuple-element.75) | copy-start | bytes 3076
  14.5 2.6 copy-start.24
  65.9 2.8 %copy-start.7 = (bf16[3840,256]{1,0:T(8,128)(2,1)S(1)}, bf16[3840,256]{1,0:T(8,128)(2,1)}, u32[]{:S(2)}) copy-start(bf16[3840,256]{1,0:T(8,128)(2,1)} %get-tuple-element.30.cat_ref) | copy-start | bytes 5898244
  66.0 1.7 copy-start.10
  66.1 0.7 copy-start.11
  66.2 1.4 copy-start.27
  66.9 1.3 copy-start.12
  67.9 0.6 copy-start.8
  97.2 4.2 %copy-start = (f32[3840,128]{1,0:T(8,128)S(1)}, f32[3840,128]{1,0:T(8,128)}, u32[]{:S(2)}) copy-start(f32[3840,128]{1,0:T(8,128)} %broadcast_in_dim.37.rating_ref) | copy-start | bytes 5898244
  100.1 34.6 %copy-start.9 = (f32[256,128]{0,1:T(8,128)}, f32[256,128]{0,1:T(8,128)S(1)}, u32[]{:S(2)}) copy-start(f32[256,128]{0,1:T(8,128)S(1)} %get-tuple-element.81) | copy-start | bytes 393220
  101.4 1.5 copy-start.1
  103.0 1.5 copy-start.4
  104.5 30.1 %copy-start.14 = (f32[256]{0:T(256)S(1)}, f32[256]{0:T(256)}, u32[]{:S(2)}) copy-start(f32[256]{0:T(256)} %copy-done.13) | copy-start | bytes 3076
  104.5 30.1 %copy-start.16 = (f32[256]{0:T(256)S(1)}, f32[256]{0:T(256)}, u32[]{:S(2)}) copy-start(f32[256]{0:T(256)} %copy-done.15) | copy-start | bytes 3076
  134.5 33.1 %copy-start.5 = (f32[3840,128]{1,0:T(8,128)}, f32[3840,128]{1,0:T(8,128)S(1)}, u32[]{:S(2)}) copy-start(f32[3840,128]{1,0:T(8,128)S(1)} %get-tuple-element.42.dual_ref) | copy-start | bytes 5898244
  134.5 0.8 copy-start.29
  135.4 32.4 %copy-start.21 = (f32[256]{0:T(256)S(1)}, f32[256]{0:T(256)}, u32[]{:S(2)}) copy-start(f32[256]{0:T(256)} %copy-done.20) | copy-start | bytes 3076
  135.4 32.4 %copy-start.23 = (f32[256]{0:T(256)S(1)}, f32[256]{0:T(256)}, u32[]{:S(2)}) copy-start(f32[256]{0:T(256)} %copy-done.22) | copy-start | bytes 3076
  135.4 32.4 %copy-start.28 = (f32[128]{0:T(128)S(1)}, f32[128]{0:T(128)}, u32[]{:S(2)}) copy-start(f32[128]{0:T(128)} %copy-done.27) | copy-start | bytes 1540
  135.4 32.7 %copy-start.19 = (f32[256]{0:T(256)S(1)}, f32[256]{0:T(256)}, u32[]{:S(2)}) copy-start(f32[256]{0:T(256)} %copy-done.18) | copy-start | bytes 3076
  170.6 1.5 copy-start.2
  172.2 1.5 copy-start.6
  173.7 30.0 %copy-start.30 = (f32[1,128]{1,0:T(1,128)S(1)}, f32[1,128]{1,0:T(1,128)}, u32[]{:S(2)}) copy-start(f32[1,128]{1,0:T(1,128)} %copy-done.29) | copy-start | bytes 1540
  173.7 30.1 %copy-start.17 = (f32[256]{0:T(256)S(1)}, f32[256]{0:T(256)}, u32[]{:S(2)}) copy-start(f32[256]{0:T(256)} %copy-done.15) | copy-start | bytes 3076
  204.1 33.1 %copy-start.3 = (f32[3840,128]{1,0:T(8,128)S(1)}, f32[3840,128]{1,0:T(8,128)}, u32[]{:S(2)}) copy-start(f32[3840,128]{1,0:T(8,128)} %get-tuple-element.33.flow_ref) | copy-start | bytes 5898244
